TPU v7x, 32 devices: a whole 2x2x4 slice. The times are simulated.
32 devices in a mesh: comp: 4 (over y, core), horiz: 2 (over x), trc: 4 (over z).
Axes of the slice: x: 2, y: 2, z: 4, core: 2. Of those that a mesh axis runs over, the one named last changes fastest.
Arguments:
- tracers: float32 [16, 64, 64, 256], P(('comp', 'trc'), None, 'horiz'), may hold values from -6 to 6
- eastward: float32 [64, 64, 256], P(('comp', 'trc'), 'horiz'), may hold values from -1.2 to 1.2
- northward: float32 [64, 64, 256], P(('comp', 'trc'), 'horiz'), may hold values from -1.2 to 1.2
- surface_height: float32 [64, 256], P('horiz'), may hold values from -6 to 6
- sea_mask: int32 [64, 256], P('horiz'), may hold values 0 or 1
- mixing: float32 [64, 64, 256], P(('comp', 'trc'), 'horiz'), may hold values from 0.02 to 0.15
- sunlight: float32 [64, 256], P('horiz'), may hold values from 0.5 to 4
- reaction: float32 [16, 16], replicated, may hold values from -1.5 to 1.5
Outputs:
- east_out: float32 [64, 64, 256], P(('comp', 'trc'), 'horiz')
- north_out: float32 [64, 64, 256], P(('comp', 'trc'), 'horiz')
- tracers_out: float32 [16, 64, 64, 256], P(None, ('comp', 'trc'), 'horiz')
- heating: float32 [64, 64, 256], P(('comp', 'trc'), 'horiz')
All inputs are finite; a program needn't handle non-finite values. No bound on the sum of `sea_mask` on one device may be relied on, other than what follows from the above.
Results may differ from a plain program's by a relative error of at most 0.00017.
Values sent between devices are 32-bit elements; how exact they have to be, the bound alone decides.
A program may use at most 64 MiB of HBM per device.

v0:
```python
import jax
import jax.numpy as jnp
from jax import lax
from jax.sharding import PartitionSpec as P

SUBSTEPS = 4


TIME_STEP = 0.25
GRAVITY = 1.0
VISCOSITY = 0.05
COURANT = 0.2
HALF_LIGHT = 0.3


def with_halo(block, sides, width):
    for axis, dim in sides:
        count = lax.axis_size(axis)
        forward = [(i, i + 1) for i in range(count - 1)]
        backward = [(target, source) for source, target in forward]
        low = lax.ppermute(
            lax.slice_in_dim(block, block.shape[dim] - width, None, axis=dim), axis, forward
        )
        high = lax.ppermute(lax.slice_in_dim(block, 0, width, axis=dim), axis, backward)
        block = jnp.concatenate([low, block, high], axis=dim)
    return block


def shifted(shard, axis, by):
    length = lax.axis_size(axis)
    pairs = [(i, i + by) for i in range(length) if 0 <= i + by < length]
    return lax.ppermute(shard, axis, pairs)


def entering(shard, axis, combine, identity):
    length, position = (lax.axis_size(axis), lax.axis_index(axis))
    everything = lax.all_gather(shard, axis)
    start = jnp.broadcast_to(jnp.asarray(identity, shard.dtype), shard.shape)

    def lap(k, before):
        reached = k < position
        new = combine(before, everything[k])
        return jnp.where(reached, new, before)

    return lax.fori_loop(0, length, lap, start)


def pad_rows(array):
    return jnp.pad(array, [(0, 0)] * (array.ndim - 1) + [(1, 1)])


def ocean_step(east_ext, north_ext, height_ext, wet_ext, mixing, bottom_keep):
    width = east_ext.shape[1] - 4
    rows = east_ext.shape[2]
    coriolis = 0.5 + 0.5 * jnp.arange(rows, dtype=jnp.float32) / rows
    east_pad = pad_rows(east_ext)
    north_pad = pad_rows(north_ext)
    height_pad = pad_rows(height_ext)
    wet_pad = pad_rows(wet_ext)
    east_mid = east_ext[:, 1 : width + 2]
    east_lap = (
        east_ext[:, 2 : width + 3]
        + east_ext[:, 0 : width + 1]
        + east_pad[:, 1 : width + 2, 2:]
        + east_pad[:, 1 : width + 2, :-2]
        - 4.0 * east_mid
    )
    north_avg = 0.25 * (
        north_pad[:, 1 : width + 2, 1:-1]
        + north_pad[:, 2 : width + 3, 1:-1]
        + north_pad[:, 1 : width + 2, :-2]
        + north_pad[:, 2 : width + 3, :-2]
    )
    slope_x = height_ext[2 : width + 3] - height_ext[1 : width + 2]
    open_x = wet_ext[1 : width + 2] * wet_ext[2 : width + 3]
    east_new = open_x * (
        east_mid + TIME_STEP * (coriolis * north_avg - GRAVITY * slope_x + VISCOSITY * east_lap)
    )
    north_mid = north_ext[:, 2 : width + 2]
    north_lap = (
        north_ext[:, 3 : width + 3]
        + north_ext[:, 1 : width + 1]
        + north_pad[:, 2 : width + 2, 2:]
        + north_pad[:, 2 : width + 2, :-2]
        - 4.0 * north_mid
    )
    east_avg = 0.25 * (
        east_pad[:, 2 : width + 2, 1:-1]
        + east_pad[:, 1 : width + 1, 1:-1]
        + east_pad[:, 2 : width + 2, 2:]
        + east_pad[:, 1 : width + 1, 2:]
    )
    slope_y = height_pad[2 : width + 2, 2:] - height_pad[2 : width + 2, 1:-1]
    open_y = wet_pad[2 : width + 2, 1:-1] * wet_pad[2 : width + 2, 2:]
    north_new = open_y * (
        north_mid + TIME_STEP * (-coriolis * east_avg - GRAVITY * slope_y + VISCOSITY * north_lap)
    )
    east_out = east_new[:, 1:]
    speed = jnp.minimum(east_out * east_out + north_new * north_new, 1.0)
    kappa = wet_ext[2 : width + 2] * mixing * (1.0 + speed) * bottom_keep
    return (east_out, north_new, COURANT * east_new, COURANT * north_new, kappa)


def advance(padded, flux_x, flux_y, kappa, kappa_up):
    inner = padded[..., 1:-1, 1:-1, :]
    level_mid = padded[..., 1:-1, :, :]
    width = inner.shape[-2]
    east_flux = (
        jnp.maximum(flux_x, 0.0) * level_mid[..., 0 : width + 1, :]
        + jnp.minimum(flux_x, 0.0) * level_mid[..., 1 : width + 2, :]
    )
    across_x = east_flux[..., :-1, :] - east_flux[..., 1:, :]
    north_cells = jnp.pad(inner[..., 1:], [(0, 0)] * (inner.ndim - 1) + [(0, 1)])
    north_flux = jnp.maximum(flux_y, 0.0) * inner + jnp.minimum(flux_y, 0.0) * north_cells
    south_flux = jnp.pad(north_flux[..., :-1], [(0, 0)] * (inner.ndim - 1) + [(1, 0)])
    across_y = south_flux - north_flux
    below = kappa * (padded[..., 2:, 1:-1, :] - inner)
    above = kappa_up * (inner - padded[..., :-2, 1:-1, :])
    return inner + across_x + across_y + below - above


def add_terms(earlier, later):
    return earlier + later


def per_device(tracers, eastward, northward, surface_height, sea_mask, mixing, sunlight, reaction):
    depth_dev = eastward.shape[0]
    groups = lax.axis_size(("comp", "trc"))
    levels = depth_dev * groups
    first_level = lax.axis_index(("comp", "trc")) * depth_dev
    keep = (first_level + jnp.arange(depth_dev) < levels - 1).astype(jnp.float32)[:, None, None]
    wet_local = sea_mask.astype(jnp.float32)
    stacked = jnp.concatenate([eastward, northward, surface_height[None], wet_local[None]], 0)
    edges = with_halo(stacked, (("horiz", 1),), 2)
    east_out, north_out, flux_x, flux_y, kappa = ocean_step(
        edges[:depth_dev],
        edges[depth_dev : 2 * depth_dev],
        edges[2 * depth_dev],
        edges[2 * depth_dev + 1],
        mixing,
        keep,
    )
    above_kappa = shifted(kappa[-1], ("comp", "trc"), 1)
    kappa_up = jnp.concatenate([above_kappa[None], kappa[:-1]], 0)
    field = lax.all_to_all(tracers, ("comp", "trc"), split_axis=1, concat_axis=0, tiled=True)
    for step in range(SUBSTEPS):
        padded = with_halo(field, ((("comp", "trc"), 1), ("horiz", 2)), 1)
        field = advance(padded, flux_x, flux_y, kappa, kappa_up)
    tau = (0.5 + field[0] * field[0]) / levels
    total = jnp.sum(tau, 0)
    above = entering(total, ("comp", "trc"), add_terms, jnp.zeros_like(total))
    depth_top = above + (jnp.cumsum(tau, 0) - tau)
    light_top = sunlight * jnp.exp(-depth_top)
    heating = levels * light_top * (1.0 - jnp.exp(-tau))
    light_mid = light_top * jnp.exp(-0.5 * tau)
    limit = light_mid / (light_mid + HALF_LIGHT)
    growth = jnp.einsum("ij,jlxy->ilxy", reaction, field, precision=lax.Precision.HIGHEST)
    tracers_out = field + limit * growth
    return (east_out, north_out, tracers_out, heating)


def solution(mesh):
    return jax.shard_map(
        per_device,
        mesh=mesh,
        in_specs=(
            P(("comp", "trc"), None, "horiz", None),
            P(("comp", "trc"), "horiz", None),
            P(("comp", "trc"), "horiz", None),
            P("horiz", None),
            P("horiz", None),
            P(("comp", "trc"), "horiz", None),
            P("horiz", None),
            P(),
        ),
        out_specs=(
            P(("comp", "trc"), "horiz", None),
            P(("comp", "trc"), "horiz", None),
            P(None, ("comp", "trc"), "horiz", None),
            P(("comp", "trc"), "horiz", None),
        ),
        check_vma=False,
    )
```

profile of v0, /device:TPU:29, one launch (start us, length us, event | category | flops | bytes accessed | tf_op | source)
XLA Modules:
  0.0 248.3 jit_solution(5421271237310587998)
XLA Ops:
  0.7 6.5 %all-to-all-start = ((f32[1,64,32,256]{3,2,0,1:T(8,128)}), f32[1,64,32,256]{3,2,0,1:T(8,128)S(1)}, u32[]{:S(2)}, u32[]{:S(2)}) async-start(f32[1,64,32,256]{3,2,0,1:T(8,128)} %bitcast.90), calls=%async_computation | async-start | bytes 4194304 | tf_op jit(solution)/shard_map/all_to_all | solution.py:145
  8.5 4.0 %collective-permute-start = (f32[10,2,256]{2,1,0:T(2,128)S(1)}, f32[10,2,256]{2,1,0:T(2,128)S(1)}, u32[]{:S(2)}, u32[]{:S(2)}) collective-permute-start(f32[10,2,256]{2,1,0:T(2,128)S(1)} %get-tuple-element.146), channel_id=1, source_target_pairs={{0,4},{1,5},{2,6},{3,7},{8,12},{9,13},{10,14},{11,15},{16,20},{17,... | collective-permute-start | bytes 61448 | tf_op jit(solution)/shard_map/ppermute | solution.py:21
  16.5 37.3 %all-to-all-done = f32[1,64,32,256]{3,2,0,1:T(8,128)S(1)} async-done(((f32[1,64,32,256]{3,2,0,1:T(8,128)}), f32[1,64,32,256]{3,2,0,1:T(8,128)S(1)}, u32[]{:S(2)}, u32[]{:S(2)}) %all-to-all-start) | async-done | bytes 2097184 | tf_op jit(solution)/shard_map/all_to_all | solution.py:145
  53.9 1.3 collective-permute-start.2
  55.2 4.0 %collective-permute-start.3 = (f32[16,1,32,256]{3,2,1,0:T(8,128)S(1)}, f32[16,1,32,256]{3,2,1,0:T(8,128)S(1)}, u32[]{:S(2)}, u32[]{:S(2)}) collective-permute-start(f32[16,1,32,256]{3,2,1,0:T(8,128)S(1)} %get-tuple-element.138), channel_id=1, source_target_pairs={{1,0},{2,1},{3,2},{8,3},{9,8},{10,9},{11,10},{16,11},{17,16},{18,1... | collective-permute-start | bytes 1572872 | tf_op jit(solution)/shard_map/ppermute | solution.py:24
  60.0 8.8 %collective-permute-done.2 = f32[16,1,32,256]{3,2,1,0:T(8,128)S(1)} collective-permute-done((f32[16,1,32,256]{3,2,1,0:T(8,128)S(1)}, f32[16,1,32,256]{3,2,1,0:T(8,128)S(1)}, u32[]{:S(2)}, u32[]{:S(2)}) %collective-permute-start.2) | collective-permute-done | bytes 524320 | tf_op jit(solution)/shard_map/ppermute | solution.py:21
  68.8 2.0 collective-permute-done.3
  71.0 3.1 %collective-permute-start.4 = (f32[16,6,1,256]{3,2,1,0:T(1,128)S(1)}, f32[16,6,1,256]{3,2,1,0:T(1,128)S(1)}, u32[]{:S(2)}, u32[]{:S(2)}) collective-permute-start(f32[16,6,1,256]{3,2,1,0:T(1,128)S(1)} %get-tuple-element.130), channel_id=1, source_target_pairs={{0,4},{1,5},{2,6},{3,7},{8,12},{9,13},{10,14},{11,15},{16,20},{17,... | collective-permute-start | bytes 294920 | tf_op jit(solution)/shard_map/ppermute | solution.py:21
  75.9 3.8 %collective-permute-done.5 = f32[16,6,1,256]{3,2,1,0:T(1,128)S(1)} collective-permute-done((f32[16,6,1,256]{3,2,1,0:T(1,128)S(1)}, f32[16,6,1,256]{3,2,1,0:T(1,128)S(1)}, u32[]{:S(2)}, u32[]{:S(2)}) %collective-permute-start.5) | collective-permute-done | bytes 98336 | tf_op jit(solution)/shard_map/ppermute | solution.py:24
  80.6 1.8 fusion.38
  83.8 7.2 %collective-permute-start.8 = (f32[16,1,32,256]{3,2,1,0:T(8,128)S(1)}, f32[16,1,32,256]{3,2,1,0:T(8,128)S(1)}, u32[]{:S(2)}, u32[]{:S(2)}) collective-permute-start(f32[16,1,32,256]{3,2,1,0:T(8,128)S(1)} %get-tuple-element.136), channel_id=1, source_target_pairs={{1,0},{2,1},{3,2},{8,3},{9,8},{10,9},{11,10},{16,11},{17,16},{18,1... | collective-permute-start | bytes 1572872 | tf_op jit(solution)/shard_map/ppermute | solution.py:24
  91.6 4.0 %collective-permute-done.7 = f32[16,1,32,256]{3,2,1,0:T(8,128)S(1)} collective-permute-done((f32[16,1,32,256]{3,2,1,0:T(8,128)S(1)}, f32[16,1,32,256]{3,2,1,0:T(8,128)S(1)}, u32[]{:S(2)}, u32[]{:S(2)}) %collective-permute-start.7) | collective-permute-done | bytes 524320 | tf_op jit(solution)/shard_map/ppermute | solution.py:21
  95.6 1.5 collective-permute-done.8
  98.5 4.0 %collective-permute-start.9 = (f32[16,6,1,256]{3,2,1,0:T(1,128)S(1)}, f32[16,6,1,256]{3,2,1,0:T(1,128)S(1)}, u32[]{:S(2)}, u32[]{:S(2)}) collective-permute-start(f32[16,6,1,256]{3,2,1,0:T(1,128)S(1)} %get-tuple-element.128), channel_id=1, source_target_pairs={{0,4},{1,5},{2,6},{3,7},{8,12},{9,13},{10,14},{11,15},{16,20},{17,... | collective-permute-start | bytes 294920 | tf_op jit(solution)/shard_map/ppermute | solution.py:21
  105.0 1.8 fusion.30
  108.2 11.1 %collective-permute-start.12 = (f32[16,1,32,256]{3,2,1,0:T(8,128)S(1)}, f32[16,1,32,256]{3,2,1,0:T(8,128)S(1)}, u32[]{:S(2)}, u32[]{:S(2)}) collective-permute-start(f32[16,1,32,256]{3,2,1,0:T(8,128)S(1)} %get-tuple-element.134), channel_id=1, source_target_pairs={{1,0},{2,1},{3,2},{8,3},{9,8},{10,9},{11,10},{16,11},{17,16},{18,1... | collective-permute-start | bytes 1572872 | tf_op jit(solution)/shard_map/ppermute | solution.py:24
  120.0 4.0 %collective-permute-done.11 = f32[16,1,32,256]{3,2,1,0:T(8,128)S(1)} collective-permute-done((f32[16,1,32,256]{3,2,1,0:T(8,128)S(1)}, f32[16,1,32,256]{3,2,1,0:T(8,128)S(1)}, u32[]{:S(2)}, u32[]{:S(2)}) %collective-permute-start.11) | collective-permute-done | bytes 524320 | tf_op jit(solution)/shard_map/ppermute | solution.py:21
  124.0 1.5 collective-permute-done.12
  125.6 3.7 %collective-permute-start.13 = (f32[16,6,1,256]{3,2,1,0:T(1,128)S(1)}, f32[16,6,1,256]{3,2,1,0:T(1,128)S(1)}, u32[]{:S(2)}, u32[]{:S(2)}) collective-permute-start(f32[16,6,1,256]{3,2,1,0:T(1,128)S(1)} %get-tuple-element.126), channel_id=1, source_target_pairs={{0,4},{1,5},{2,6},{3,7},{8,12},{9,13},{10,14},{11,15},{16,20},{17,... | collective-permute-start | bytes 294920 | tf_op jit(solution)/shard_map/ppermute | solution.py:21
  131.4 3.6 %collective-permute-done.14 = f32[16,6,1,256]{3,2,1,0:T(1,128)S(1)} collective-permute-done((f32[16,6,1,256]{3,2,1,0:T(1,128)S(1)}, f32[16,6,1,256]{3,2,1,0:T(1,128)S(1)}, u32[]{:S(2)}, u32[]{:S(2)}) %collective-permute-start.14) | collective-permute-done | bytes 98336 | tf_op jit(solution)/shard_map/ppermute | solution.py:24
  135.8 1.8 fusion.22
  140.0 11.2 %collective-permute-start.16 = (f32[16,1,32,256]{3,2,1,0:T(8,128)}, f32[16,1,32,256]{3,2,1,0:T(8,128)S(1)}, u32[]{:S(2)}, u32[]{:S(2)}) collective-permute-start(f32[16,1,32,256]{3,2,1,0:T(8,128)} %get-tuple-element.132), channel_id=1, source_target_pairs={{1,0},{2,1},{3,2},{8,3},{9,8},{10,9},{11,10},{16,11},{17,16},{18,1... | collective-permute-start | bytes 1572872 | tf_op jit(solution)/shard_map/ppermute | solution.py:24
  151.8 4.5 %collective-permute-done.15 = f32[16,1,32,256]{3,2,1,0:T(8,128)S(1)} collective-permute-done((f32[16,1,32,256]{3,2,1,0:T(8,128)}, f32[16,1,32,256]{3,2,1,0:T(8,128)S(1)}, u32[]{:S(2)}, u32[]{:S(2)}) %collective-permute-start.15) | collective-permute-done | bytes 524320 | tf_op jit(solution)/shard_map/ppermute | solution.py:21
  157.7 1.5 collective-permute-start.17
  159.3 1.6 collective-permute-start.18
  161.4 3.3 %collective-permute-done.18 = f32[16,6,1,256]{3,2,1,0:T(1,128)S(1)} collective-permute-done((f32[16,6,1,256]{3,2,1,0:T(1,128)S(1)}, f32[16,6,1,256]{3,2,1,0:T(1,128)S(1)}, u32[]{:S(2)}, u32[]{:S(2)}) %collective-permute-start.18) | collective-permute-done | bytes 98336 | tf_op jit(solution)/shard_map/ppermute | solution.py:24
  165.6 1.8 fusion.14
  167.4 1.3 copy-done.1
  168.8 68.8 %all-gather = f32[512,256]{1,0:T(8,128)S(1)} all-gather(f32[32,256]{1,0:T(8,128)S(1)} %fusion.91), channel_id=2, replica_groups=mesh['comp'=4,'horiz'=2,'trc'=4] {'comp','trc'}, dimensions={0}, use_global_device_ids=true | all-gather | bytes 557056 | tf_op jit(solution)/shard_map/all_gather | solution.py:37
  238.2 1.7 fusion.84
  240.9 4.7 %fusion.44 = f32[4,32,256,16]{2,3,1,0:T(8,128)S(1)} fusion(f32[16,4,32,256]{3,2,1,0:T(8,128)} %copy-done.1, f32[16,16]{1,0:T(8,128)S(1)} %copy-done), kind=kOutput, calls=%fused_computation.83 | convolution fusion | flops 100663296 | bytes 4195328 | tf_op jit(solution)/shard_map/ij,jlxy->ilxy/dot_general | solution.py:157
  245.7 2.6 %bitcast_add_fusion = f32[16,4,32,256]{3,2,1,0:T(8,128)} fusion(f32[16,4,32,256]{3,2,1,0:T(8,128)S(1)} %copy-done.2, f32[4,32,256,16]{2,3,1,0:T(8,128)S(1)} %fusion.44, f32[4,32,256]{2,1,0:T(8,128)S(1)} %fusion.58), kind=kLoop, calls=%fused_computation.81 | loop fusion | flops 1048576 | bytes 6422528 | tf_op jit(solution)/shard_map/add | solution.py:158
  (111 shorter events, 27.1 us)
Async XLA Ops:
  0.6 240.3 %copy-start = (f32[16,16]{1,0:T(8,128)S(1)}, f32[16,16]{1,0:T(8,128)}, u32[]{:S(2)}) copy-start(f32[16,16]{1,0:T(8,128)} %param.17) | copy-start | bytes 3076
  0.7 6.5 %copy-start.3 = (f32[4,32,256]{2,1,0:T(8,128)S(1)}, f32[4,32,256]{2,1,0:T(8,128)}, u32[]{:S(2)}) copy-start(f32[4,32,256]{2,1,0:T(8,128)} %param.12) | copy-start | bytes 393220
  0.7 6.5 %copy-start.4 = (f32[4,32,256]{2,1,0:T(8,128)S(1)}, f32[4,32,256]{2,1,0:T(8,128)}, u32[]{:S(2)}) copy-start(f32[4,32,256]{2,1,0:T(8,128)} %param.11) | copy-start | bytes 393220
  0.7 6.5 %copy-start.13 = (f32[32,256]{1,0:T(8,128)S(1)}, f32[32,256]{1,0:T(8,128)}, u32[]{:S(2)}) copy-start(f32[32,256]{1,0:T(8,128)} %param.13) | copy-start | bytes 98308
  0.7 53.1 %all-to-all-start = ((f32[1,64,32,256]{3,2,0,1:T(8,128)}), f32[1,64,32,256]{3,2,0,1:T(8,128)S(1)}, u32[]{:S(2)}, u32[]{:S(2)}) async-start(f32[1,64,32,256]{3,2,0,1:T(8,128)} %bitcast.90), calls=%async_computation | async-start | bytes 4194304 | tf_op jit(solution)/shard_map/all_to_all | solution.py:145
  7.2 5.3 %collective-permute-start.1 = (f32[10,2,256]{2,1,0:T(2,128)S(1)}, f32[10,2,256]{2,1,0:T(2,128)S(1)}, u32[]{:S(2)}, u32[]{:S(2)}) collective-permute-start(f32[10,2,256]{2,1,0:T(2,128)S(1)} %get-tuple-element.147), channel_id=1, source_target_pairs={{4,0},{5,1},{6,2},{7,3},{12,8},{13,9},{14,10},{15,11},{20,16},{21,... | collective-permute-start | bytes 61448 | tf_op jit(solution)/shard_map/ppermute | solution.py:24
  8.5 4.9 %collective-permute-start = (f32[10,2,256]{2,1,0:T(2,128)S(1)}, f32[10,2,256]{2,1,0:T(2,128)S(1)}, u32[]{:S(2)}, u32[]{:S(2)}) collective-permute-start(f32[10,2,256]{2,1,0:T(2,128)S(1)} %get-tuple-element.146), channel_id=1, source_target_pairs={{0,4},{1,5},{2,6},{3,7},{8,12},{9,13},{10,14},{11,15},{16,20},{17,... | collective-permute-start | bytes 61448 | tf_op jit(solution)/shard_map/ppermute | solution.py:21
  14.0 121.0 %copy-start.5 = (f32[4,33,256]{2,1,0:T(8,128)}, f32[4,33,256]{2,1,0:T(8,128)S(1)}, u32[]{:S(2)}) copy-start(f32[4,33,256]{2,1,0:T(8,128)S(1)} %get-tuple-element.122) | copy-start | bytes 405508
  15.2 44.8 %copy-start.14 = (f32[4,32,256]{2,1,0:T(8,128)}, f32[4,32,256]{2,1,0:T(8,128)S(1)}, u32[]{:S(2)}) copy-start(f32[4,32,256]{2,1,0:T(8,128)S(1)} %get-tuple-element.120) | copy-start | bytes 393220
  15.2 44.1 %collective-permute-start.6 = (f32[32,256]{1,0:T(8,128)S(1)}, f32[32,256]{1,0:T(8,128)S(1)}, u32[]{:S(2)}, u32[]{:S(2)}) collective-permute-start(f32[32,256]{1,0:T(8,128)S(1)} %slice_bitcast_fusion), channel_id=1, source_target_pairs={{0,1},{1,2},{2,3},{3,8},{8,9},{9,10},{10,11},{11,16},{16,17},{17,1... | collective-permute-start | bytes 98312 | tf_op jit(solution)/shard_map/ppermute | solution.py:32
  53.9 14.9 %collective-permute-start.2 = (f32[16,1,32,256]{3,2,1,0:T(8,128)S(1)}, f32[16,1,32,256]{3,2,1,0:T(8,128)S(1)}, u32[]{:S(2)}, u32[]{:S(2)}) collective-permute-start(f32[16,1,32,256]{3,2,1,0:T(8,128)S(1)} %get-tuple-element.139), channel_id=1, source_target_pairs={{0,1},{1,2},{2,3},{3,8},{8,9},{9,10},{10,11},{11,16},{16,17},{17,1... | collective-permute-start | bytes 1572872 | tf_op jit(solution)/shard_map/ppermute | solution.py:21
  55.2 15.6 %collective-permute-start.3 = (f32[16,1,32,256]{3,2,1,0:T(8,128)S(1)}, f32[16,1,32,256]{3,2,1,0:T(8,128)S(1)}, u32[]{:S(2)}, u32[]{:S(2)}) collective-permute-start(f32[16,1,32,256]{3,2,1,0:T(8,128)S(1)} %get-tuple-element.138), channel_id=1, source_target_pairs={{1,0},{2,1},{3,2},{8,3},{9,8},{10,9},{11,10},{16,11},{17,16},{18,1... | collective-permute-start | bytes 1572872 | tf_op jit(solution)/shard_map/ppermute | solution.py:24
  59.3 71.4 %copy-start.9 = (f32[4,32,256]{2,1,0:T(8,128)}, f32[4,32,256]{2,1,0:T(8,128)S(1)}, u32[]{:S(2)}) copy-start(f32[4,32,256]{2,1,0:T(8,128)S(1)} %get-tuple-element.148) | copy-start | bytes 393220
  59.3 71.4 %copy-start.11 = (f32[4,32,256]{2,1,0:T(8,128)}, f32[4,32,256]{2,1,0:T(8,128)S(1)}, u32[]{:S(2)}) copy-start(f32[4,32,256]{2,1,0:T(8,128)S(1)} %get-tuple-element.149) | copy-start | bytes 393220
  59.4 76.5 %copy-start.7 = (f32[4,32,256]{2,1,0:T(8,128)}, f32[4,32,256]{2,1,0:T(8,128)S(1)}, u32[]{:S(2)}) copy-start(f32[4,32,256]{2,1,0:T(8,128)S(1)} %pad_maximum_fusion.34) | copy-start | bytes 393220
  71.0 4.9 %collective-permute-start.4 = (f32[16,6,1,256]{3,2,1,0:T(1,128)S(1)}, f32[16,6,1,256]{3,2,1,0:T(1,128)S(1)}, u32[]{:S(2)}, u32[]{:S(2)}) collective-permute-start(f32[16,6,1,256]{3,2,1,0:T(1,128)S(1)} %get-tuple-element.130), channel_id=1, source_target_pairs={{0,4},{1,5},{2,6},{3,7},{8,12},{9,13},{10,14},{11,15},{16,20},{17,... | collective-permute-start | bytes 294920 | tf_op jit(solution)/shard_map/ppermute | solution.py:21
  74.1 5.7 %collective-permute-start.5 = (f32[16,6,1,256]{3,2,1,0:T(1,128)S(1)}, f32[16,6,1,256]{3,2,1,0:T(1,128)S(1)}, u32[]{:S(2)}, u32[]{:S(2)}) collective-permute-start(f32[16,6,1,256]{3,2,1,0:T(1,128)S(1)} %get-tuple-element.131), channel_id=1, source_target_pairs={{4,0},{5,1},{6,2},{7,3},{12,8},{13,9},{14,10},{15,11},{20,16},{21,... | collective-permute-start | bytes 294920 | tf_op jit(solution)/shard_map/ppermute | solution.py:24
  82.5 13.1 %collective-permute-start.7 = (f32[16,1,32,256]{3,2,1,0:T(8,128)S(1)}, f32[16,1,32,256]{3,2,1,0:T(8,128)S(1)}, u32[]{:S(2)}, u32[]{:S(2)}) collective-permute-start(f32[16,1,32,256]{3,2,1,0:T(8,128)S(1)} %get-tuple-element.137), channel_id=1, source_target_pairs={{0,1},{1,2},{2,3},{3,8},{8,9},{9,10},{10,11},{11,16},{16,17},{17,1... | collective-permute-start | bytes 1572872 | tf_op jit(solution)/shard_map/ppermute | solution.py:21
  83.8 13.3 %collective-permute-start.8 = (f32[16,1,32,256]{3,2,1,0:T(8,128)S(1)}, f32[16,1,32,256]{3,2,1,0:T(8,128)S(1)}, u32[]{:S(2)}, u32[]{:S(2)}) collective-permute-start(f32[16,1,32,256]{3,2,1,0:T(8,128)S(1)} %get-tuple-element.136), channel_id=1, source_target_pairs={{1,0},{2,1},{3,2},{8,3},{9,8},{10,9},{11,10},{16,11},{17,16},{18,1... | collective-permute-start | bytes 1572872 | tf_op jit(solution)/shard_map/ppermute | solution.py:24
  97.2 5.8 %collective-permute-start.10 = (f32[16,6,1,256]{3,2,1,0:T(1,128)S(1)}, f32[16,6,1,256]{3,2,1,0:T(1,128)S(1)}, u32[]{:S(2)}, u32[]{:S(2)}) collective-permute-start(f32[16,6,1,256]{3,2,1,0:T(1,128)S(1)} %get-tuple-element.129), channel_id=1, source_target_pairs={{4,0},{5,1},{6,2},{7,3},{12,8},{13,9},{14,10},{15,11},{20,16},{21,... | collective-permute-start | bytes 294920 | tf_op jit(solution)/shard_map/ppermute | solution.py:24
  98.5 5.6 %collective-permute-start.9 = (f32[16,6,1,256]{3,2,1,0:T(1,128)S(1)}, f32[16,6,1,256]{3,2,1,0:T(1,128)S(1)}, u32[]{:S(2)}, u32[]{:S(2)}) collective-permute-start(f32[16,6,1,256]{3,2,1,0:T(1,128)S(1)} %get-tuple-element.128), channel_id=1, source_target_pairs={{0,4},{1,5},{2,6},{3,7},{8,12},{9,13},{10,14},{11,15},{16,20},{17,... | collective-permute-start | bytes 294920 | tf_op jit(solution)/shard_map/ppermute | solution.py:21
  106.9 17.1 %collective-permute-start.11 = (f32[16,1,32,256]{3,2,1,0:T(8,128)S(1)}, f32[16,1,32,256]{3,2,1,0:T(8,128)S(1)}, u32[]{:S(2)}, u32[]{:S(2)}) collective-permute-start(f32[16,1,32,256]{3,2,1,0:T(8,128)S(1)} %get-tuple-element.135), channel_id=1, source_target_pairs={{0,1},{1,2},{2,3},{3,8},{8,9},{9,10},{10,11},{11,16},{16,17},{17,1... | collective-permute-start | bytes 1572872 | tf_op jit(solution)/shard_map/ppermute | solution.py:21
  108.2 17.2 %collective-permute-start.12 = (f32[16,1,32,256]{3,2,1,0:T(8,128)S(1)}, f32[16,1,32,256]{3,2,1,0:T(8,128)S(1)}, u32[]{:S(2)}, u32[]{:S(2)}) collective-permute-start(f32[16,1,32,256]{3,2,1,0:T(8,128)S(1)} %get-tuple-element.134), channel_id=1, source_target_pairs={{1,0},{2,1},{3,2},{8,3},{9,8},{10,9},{11,10},{16,11},{17,16},{18,1... | collective-permute-start | bytes 1572872 | tf_op jit(solution)/shard_map/ppermute | solution.py:24
  125.6 5.8 %collective-permute-start.13 = (f32[16,6,1,256]{3,2,1,0:T(1,128)S(1)}, f32[16,6,1,256]{3,2,1,0:T(1,128)S(1)}, u32[]{:S(2)}, u32[]{:S(2)}) collective-permute-start(f32[16,6,1,256]{3,2,1,0:T(1,128)S(1)} %get-tuple-element.126), channel_id=1, source_target_pairs={{0,4},{1,5},{2,6},{3,7},{8,12},{9,13},{10,14},{11,15},{16,20},{17,... | collective-permute-start | bytes 294920 | tf_op jit(solution)/shard_map/ppermute | solution.py:21
  129.3 5.7 %collective-permute-start.14 = (f32[16,6,1,256]{3,2,1,0:T(1,128)S(1)}, f32[16,6,1,256]{3,2,1,0:T(1,128)S(1)}, u32[]{:S(2)}, u32[]{:S(2)}) collective-permute-start(f32[16,6,1,256]{3,2,1,0:T(1,128)S(1)} %get-tuple-element.127), channel_id=1, source_target_pairs={{4,0},{5,1},{6,2},{7,3},{12,8},{13,9},{14,10},{15,11},{20,16},{21,... | collective-permute-start | bytes 294920 | tf_op jit(solution)/shard_map/ppermute | solution.py:24
  138.7 17.6 %collective-permute-start.15 = (f32[16,1,32,256]{3,2,1,0:T(8,128)}, f32[16,1,32,256]{3,2,1,0:T(8,128)S(1)}, u32[]{:S(2)}, u32[]{:S(2)}) collective-permute-start(f32[16,1,32,256]{3,2,1,0:T(8,128)} %get-tuple-element.133), channel_id=1, source_target_pairs={{0,1},{1,2},{2,3},{3,8},{8,9},{9,10},{10,11},{11,16},{16,17},{17,1... | collective-permute-start | bytes 1572872 | tf_op jit(solution)/shard_map/ppermute | solution.py:21
  140.0 17.6 %collective-permute-start.16 = (f32[16,1,32,256]{3,2,1,0:T(8,128)}, f32[16,1,32,256]{3,2,1,0:T(8,128)S(1)}, u32[]{:S(2)}, u32[]{:S(2)}) collective-permute-start(f32[16,1,32,256]{3,2,1,0:T(8,128)} %get-tuple-element.132), channel_id=1, source_target_pairs={{1,0},{2,1},{3,2},{8,3},{9,8},{10,9},{11,10},{16,11},{17,16},{18,1... | collective-permute-start | bytes 1572872 | tf_op jit(solution)/shard_map/ppermute | solution.py:24
  151.8 9.1 %copy-start.10 = (f32[4,32,256]{2,1,0:T(8,128)S(1)}, f32[4,32,256]{2,1,0:T(8,128)}, u32[]{:S(2)}) copy-start(f32[4,32,256]{2,1,0:T(8,128)} %copy-done.9) | copy-start | bytes 393220
  151.8 9.1 %copy-start.12 = (f32[4,32,256]{2,1,0:T(8,128)S(1)}, f32[4,32,256]{2,1,0:T(8,128)}, u32[]{:S(2)}) copy-start(f32[4,32,256]{2,1,0:T(8,128)} %copy-done.11) | copy-start | bytes 393220
  157.7 3.7 %collective-permute-start.17 = (f32[16,6,1,256]{3,2,1,0:T(1,128)S(1)}, f32[16,6,1,256]{3,2,1,0:T(1,128)S(1)}, u32[]{:S(2)}, u32[]{:S(2)}) collective-permute-start(f32[16,6,1,256]{3,2,1,0:T(1,128)S(1)} %get-tuple-element.124), channel_id=1, source_target_pairs={{0,4},{1,5},{2,6},{3,7},{8,12},{9,13},{10,14},{11,15},{16,20},{17,... | collective-permute-start | bytes 294920 | tf_op jit(solution)/shard_map/ppermute | solution.py:21
  159.3 5.5 %collective-permute-start.18 = (f32[16,6,1,256]{3,2,1,0:T(1,128)S(1)}, f32[16,6,1,256]{3,2,1,0:T(1,128)S(1)}, u32[]{:S(2)}, u32[]{:S(2)}) collective-permute-start(f32[16,6,1,256]{3,2,1,0:T(1,128)S(1)} %get-tuple-element.125), channel_id=1, source_target_pairs={{4,0},{5,1},{6,2},{7,3},{12,8},{13,9},{14,10},{15,11},{20,16},{21,... | collective-permute-start | bytes 294920 | tf_op jit(solution)/shard_map/ppermute | solution.py:24
  165.6 72.6 %copy-start.15 = (f32[32,256]{1,0:T(8,128)S(1)}, f32[32,256]{1,0:T(8,128)}, u32[]{:S(2)}) copy-start(f32[32,256]{1,0:T(8,128)} %param.16) | copy-start | bytes 98308
  (6 other events, 23.2 us)
where the time goes:
time: 253 us; the launch traced here: 248 us
  waiting for transfers between devices  77.6 us (31%)
  starting transfers between devices  69.6 us (28%)
  blocking collectives  68.8 us (27%)
  other arithmetic  20.3 us (8%)
  local copies, waits for them, and re-layouts  5.49 us (2%)
  matrix products  4.72 us (2%)
    all_gather x1, blocking collectives, entering(): everything = lax.all_gather(shard, axis)  68.8 us
    ppermute x9, starting transfers between devices, with_halo(): lax.ppermute(lax.slice_in_dim(block, 0, width, axis=dim), axis, backward)  40.3 us
    all_to_all x1, waiting for transfers between devices, per_device(): lax.all_to_all(tracers, ('comp', 'trc'), split_axis=1, concat_axis=0, til...  37.3 us
    ppermute x9, waiting for transfers between devices, with_halo(): lax.ppermute(lax.slice_in_dim(block, block.shape[dim] - width, None, axis...  23.2 us
    ppermute x9, starting transfers between devices, with_halo(): lax.ppermute(lax.slice_in_dim(block, block.shape[dim] - width, None, axis...  21.5 us
    ppermute x9, waiting for transfers between devices, with_halo(): lax.ppermute(lax.slice_in_dim(block, 0, width, axis=dim), axis, backward)  17.1 us
    sub x4, other arithmetic, advance(): return inner + across_x + across_y + below - above  7.21 us
    all_to_all x1, starting transfers between devices, per_device(): lax.all_to_all(tracers, ('comp', 'trc'), split_axis=1, concat_axis=0, til...  6.47 us
  transfers between devices with their start and end apart: 20, of which 14 were waited for; matrix products, arithmetic and copies ran while one was open for 2% of the time, Pallas kernels for 0%

commit v1 on v0

v1 whole, which is shorter than its diff:
```python
import functools

import jax
import jax.numpy as jnp
from jax import lax
from jax.experimental import pallas as pl
from jax.experimental.pallas import tpu as pltpu
from jax.sharding import PartitionSpec as P

SUBSTEPS = 4


TIME_STEP = 0.25
GRAVITY = 1.0
VISCOSITY = 0.05
COURANT = 0.2
HALF_LIGHT = 0.3


def with_halo(block, sides, width):
    for axis, dim in sides:
        count = lax.axis_size(axis)
        forward = [(i, i + 1) for i in range(count - 1)]
        backward = [(target, source) for source, target in forward]
        low = lax.ppermute(
            lax.slice_in_dim(block, block.shape[dim] - width, None, axis=dim), axis, forward
        )
        high = lax.ppermute(lax.slice_in_dim(block, 0, width, axis=dim), axis, backward)
        block = jnp.concatenate([low, block, high], axis=dim)
    return block


def pad_rows(array):
    return jnp.pad(array, [(0, 0)] * (array.ndim - 1) + [(1, 1)])


def ocean_step(east_ext, north_ext, height_ext, wet_ext, mixing, bottom_keep):
    width = east_ext.shape[1] - 4
    rows = east_ext.shape[2]
    coriolis = 0.5 + 0.5 * jnp.arange(rows, dtype=jnp.float32) / rows
    east_pad = pad_rows(east_ext)
    north_pad = pad_rows(north_ext)
    height_pad = pad_rows(height_ext)
    wet_pad = pad_rows(wet_ext)
    east_mid = east_ext[:, 1 : width + 2]
    east_lap = (
        east_ext[:, 2 : width + 3]
        + east_ext[:, 0 : width + 1]
        + east_pad[:, 1 : width + 2, 2:]
        + east_pad[:, 1 : width + 2, :-2]
        - 4.0 * east_mid
    )
    north_avg = 0.25 * (
        north_pad[:, 1 : width + 2, 1:-1]
        + north_pad[:, 2 : width + 3, 1:-1]
        + north_pad[:, 1 : width + 2, :-2]
        + north_pad[:, 2 : width + 3, :-2]
    )
    slope_x = height_ext[2 : width + 3] - height_ext[1 : width + 2]
    open_x = wet_ext[1 : width + 2] * wet_ext[2 : width + 3]
    east_new = open_x * (
        east_mid + TIME_STEP * (coriolis * north_avg - GRAVITY * slope_x + VISCOSITY * east_lap)
    )
    north_mid = north_ext[:, 2 : width + 2]
    north_lap = (
        north_ext[:, 3 : width + 3]
        + north_ext[:, 1 : width + 1]
        + north_pad[:, 2 : width + 2, 2:]
        + north_pad[:, 2 : width + 2, :-2]
        - 4.0 * north_mid
    )
    east_avg = 0.25 * (
        east_pad[:, 2 : width + 2, 1:-1]
        + east_pad[:, 1 : width + 1, 1:-1]
        + east_pad[:, 2 : width + 2, 2:]
        + east_pad[:, 1 : width + 1, 2:]
    )
    slope_y = height_pad[2 : width + 2, 2:] - height_pad[2 : width + 2, 1:-1]
    open_y = wet_pad[2 : width + 2, 1:-1] * wet_pad[2 : width + 2, 2:]
    north_new = open_y * (
        north_mid + TIME_STEP * (-coriolis * east_avg - GRAVITY * slope_y + VISCOSITY * north_lap)
    )
    east_out = east_new[:, 1:]
    speed = jnp.minimum(east_out * east_out + north_new * north_new, 1.0)
    kappa = wet_ext[2 : width + 2] * mixing * (1.0 + speed) * bottom_keep
    return (east_out, north_new, COURANT * east_new, COURANT * north_new, kappa)


TILE = 8
MESH = pl.DeviceIdType.MESH


def remote(src, dst, send, recv, device):
    return pltpu.make_async_remote_copy(
        src_ref=src, dst_ref=dst, send_sem=send, recv_sem=recv, device_id=device, device_id_type=MESH
    )


def kernel(
    dims, tr, coef, sun, react, out, heat,
    T, side, F, CF, tot, totr, pre, abv,
    ts, tl, trs, cs, cr, ks, kr, hs, hr, zs, zr, us, ur, bs, br,
):
    C, H, Z, levels = dims
    c, h, z = (lax.axis_index(a) for a in ("comp", "horiz", "trc"))
    group = coef.shape[1]
    deep = group * Z
    rows, wide = tr.shape[2], T.shape[3]
    cols = tr.shape[3]
    has_left, has_right = h > 0, h < H - 1

    def greet(device):
        pl.semaphore_signal(pltpu.get_barrier_semaphore(), inc=1, device_id=device, device_id_type=MESH)

    for d in range(C):
        c2 = lax.rem(c + d, C)
        if d:
            greet((c2, h, z))
        pl.when(has_left)(functools.partial(greet, (c2, h - 1, z)))
        pl.when(has_right)(functools.partial(greet, (c2, h + 1, z)))
    for d in range(1, Z):
        greet((c, h, lax.rem(z + d, Z)))
    near = has_left.astype(jnp.int32) + has_right.astype(jnp.int32)
    pl.semaphore_wait(pltpu.get_barrier_semaphore(), C * (1 + near) - 1 + Z - 1)

    def coef_copy(up, block):
        where = pl.ds(1 + block * group, group)
        src = CF.at[:, where]
        return remote(src, CF.at[:, where], cs.at[up, block], cr.at[block], (c, h, z + 1 if up else z - 1))

    CF[:, pl.ds(1 + z * group, group)] = coef[...]
    pl.when(z < Z - 1)(lambda: coef_copy(1, z).start())
    pl.when(z > 0)(lambda: coef_copy(0, z).start())

    def tracer_copies(target, source, partner):
        low, high = int(target > 0), int(target < C - 1)
        count = deep + low + high
        src = pl.ds(target * deep - low, count)
        dst = pl.ds(1 - low, count)
        middle = (tr.at[0, src], T.at[0, source, dst, pl.ds(0, rows)])
        left = remote(
            tr.at[0, src, pl.ds(rows - TILE, TILE)], side.at[0, source, dst],
            ts.at[target, 1], trs.at[source, 1], (partner, h + 1, z))
        right = remote(
            tr.at[0, src, pl.ds(0, TILE)], side.at[1, source, dst],
            ts.at[target, 2], trs.at[source, 2], (partner, h - 1, z))
        here = pltpu.make_async_copy(*middle, tl.at[0])
        there = remote(*middle, ts.at[target, 0], trs.at[source, 0], (partner, h, z))
        return here, there, left, right

    for c2 in range(C):
        here, there, left, right = tracer_copies(c2, c, c2)
        pl.when(c == c2)(here.start)
        pl.when(c != c2)(there.start)
        pl.when(has_right)(left.start)
        pl.when(has_left)(right.start)

    @pl.when(h == 0)
    def _():
        side[0] = jnp.zeros(side.shape[1:], jnp.float32)

    @pl.when(h == H - 1)
    def _():
        side[1] = jnp.zeros(side.shape[1:], jnp.float32)

    @pl.when(c == 0)
    def _():
        CF[2, 0] = jnp.zeros((wide, cols), jnp.float32)
        for s in range(SUBSTEPS):
            for k in range(C):
                T[s, k, 0] = jnp.zeros((wide, cols), jnp.float32)
        for k in range(C):
            side[0, k, 0] = jnp.zeros((TILE, cols), jnp.float32)
            side[1, k, 0] = jnp.zeros((TILE, cols), jnp.float32)

    @pl.when(c == C - 1)
    def _():
        for s in range(SUBSTEPS):
            for k in range(C):
                T[s, k, deep + 1] = jnp.zeros((wide, cols), jnp.float32)
        for k in range(C):
            side[0, k, deep + 1] = jnp.zeros((TILE, cols), jnp.float32)
            side[1, k, deep + 1] = jnp.zeros((TILE, cols), jnp.float32)

    for d in range(1, Z):
        @pl.when(z >= d)
        def _():
            coef_copy(1, z - d).wait_recv()
            pl.when(z < Z - 1)(lambda: coef_copy(1, z - d).start())

        @pl.when(z + d < Z)
        def _():
            coef_copy(0, z + d).wait_recv()
            pl.when(z > 0)(lambda: coef_copy(0, z + d).start())

    kup = remote(CF.at[2, deep], CF.at[2, 0], ks.at[0], kr.at[0], (c + 1, h, z))
    pl.when(c < C - 1)(kup.start)
    pl.when(c > 0)(kup.wait_recv)

    def halo(s, k):
        down = remote(T.at[s, k, deep], T.at[s, k, 0], hs.at[s, k, 0], hr.at[s, k, 0], (c + 1, h, z))
        up = remote(T.at[s, k, 1], T.at[s, k, deep + 1], hs.at[s, k, 1], hr.at[s, k, 1], (c - 1, h, z))
        return down, up

    def deliver(k, target, source):
        return remote(
            T.at[SUBSTEPS, k, pl.ds(1 + target * group, group), pl.ds(0, rows)], F.at[k * Z + source],
            zs.at[k, target], zr.at[k, source], (c, h, target))

    def total_copy(target, source):
        return remote(tot, totr.at[source], us.at[target], ur.at[source], (target, h, z))

    def above_copy(target):
        return remote(pre.at[target], abv, bs.at[target], br.at[0], (c, h, target))

    sub = lax.broadcasted_iota(jnp.int32, (TILE, cols), 0)

    def arrive(k):
        for cc in range(C):
            @pl.when(c == cc)
            def _():
                here, there, left, right = tracer_copies(cc, k, cc)
                pl.when(k == cc)(here.wait)
                pl.when(k != cc)(there.wait_recv)
                pl.when(has_left)(left.wait_recv)
                pl.when(has_right)(right.wait_recv)

        @pl.loop(0, deep + 2)
        def _(l):
            T[0, k, l, pl.ds(rows, TILE)] = jnp.where(sub < TILE // 2, side[1, k, l], side[0, k, l])

    def optics(m):
        return (0.5 + m * m) / levels

    def light_totals():
        run = jnp.zeros((rows, cols), jnp.float32)
        for block in range(Z):
            pre[block] = run
            for l in range(group):
                run = run + optics(T[SUBSTEPS, 0, 1 + block * group + l, pl.ds(0, rows)])
        tot[...] = run
        for c2 in range(1, C):
            pl.when(c < c2)(total_copy(c2, c).start)

    def light_above():
        base = jnp.zeros((rows, cols), jnp.float32)
        abv[...] = base
        for c2 in range(C - 1):
            @pl.when(c > c2)
            def _():
                total_copy(c, c2).wait_recv()
                abv[...] += totr[c2]
        for block in range(1, Z):
            pre[block] = pre[block] + abv[...]
            above_copy(block).start()

    def work(index, carry):
        s, k = index // C, lax.rem(index, C)
        pl.when(s == 0)(functools.partial(arrive, k))

        @pl.when(s > 0)
        def _():
            down, up = halo(s, k)
            pl.when(c > 0)(down.wait_recv)
            pl.when(c < C - 1)(up.wait_recv)

        pl.when((s == SUBSTEPS - 1) & (k == C - 1) & (z == 0))(light_above)

        def level(l, carry):
            up, mid, down = T[s, k, l], T[s, k, l + 1], T[s, k, l + 2]
            fx, fy = CF[0, l + 1], CF[1, l + 1]
            E = jnp.maximum(fx, 0.0) * mid + jnp.minimum(fx, 0.0) * pltpu.roll(mid, wide - 1, 0)
            N = jnp.maximum(fy, 0.0) * mid + jnp.minimum(fy, 0.0) * pltpu.roll(mid, cols - 1, 1)
            T[s + 1, k, l + 1] = (
                mid + (pltpu.roll(E, 1, 0) - E) + (pltpu.roll(N, 1, 1) - N)
                + CF[2, l + 1] * (down - mid) - CF[2, l] * (mid - up)
            )
            return carry

        lax.fori_loop(0, deep, level, 0)

        @pl.when(s < SUBSTEPS - 1)
        def _():
            down, up = halo(s + 1, k)
            pl.when(c < C - 1)(down.start)
            pl.when(c > 0)(up.start)

        @pl.when(s == SUBSTEPS - 1)
        def _():
            for d in range(1, Z):
                deliver(k, lax.rem(z + d, Z), z).start()
            F[k * Z + z] = T[SUBSTEPS, k, pl.ds(1 + z * group, group), pl.ds(0, rows)]
            pl.when((k == 0) & (z == 0))(light_totals)

        return carry

    lax.fori_loop(0, SUBSTEPS * C, work, 0)

    pl.when(z > 0)(above_copy(z).wait_recv)
    for k in range(C):
        for d in range(1, Z):
            deliver(k, z, lax.rem(z + d, Z)).wait_recv()

    def react_tile(index, carry):
        l, r = index // (rows // TILE), lax.rem(index, rows // TILE)
        here = pl.ds(pl.multiple_of(r * TILE, TILE), TILE)
        field = [F[j, l, here] for j in range(F.shape[0])]
        tau = optics(field[0])
        depth = abv[here]
        abv[here] = depth + tau
        light_top = sun[here] * jnp.exp(-depth)
        heat[l, here] = levels * light_top * (1.0 - jnp.exp(-tau))
        light_mid = light_top * jnp.exp(-0.5 * tau)
        limit = light_mid / (light_mid + HALF_LIGHT)
        for i in range(F.shape[0]):
            growth = react[i, 0] * field[0]
            for j in range(1, F.shape[0]):
                growth = growth + react[i, j] * field[j]
            out[i, l, here] = field[i] + limit * growth
        return carry

    lax.fori_loop(0, group * (rows // TILE), react_tile, 0)

    pl.when(z < Z - 1)(lambda: coef_copy(1, z).wait_send())
    pl.when(z > 0)(lambda: coef_copy(0, z).wait_send())
    for d in range(1, Z):
        pl.when((z >= d) & (z < Z - 1))(lambda: coef_copy(1, z - d).wait_send())
        pl.when((z + d < Z) & (z > 0))(lambda: coef_copy(0, z + d).wait_send())
    for c2 in range(C):
        here, there, left, right = tracer_copies(c2, c, c2)
        pl.when(c != c2)(there.wait_send)
        pl.when(has_right)(left.wait_send)
        pl.when(has_left)(right.wait_send)
    pl.when(c < C - 1)(kup.wait_send)
    for s in range(1, SUBSTEPS):
        for k in range(C):
            down, up = halo(s, k)
            pl.when(c < C - 1)(down.wait_send)
            pl.when(c > 0)(up.wait_send)
    for k in range(C):
        for d in range(1, Z):
            deliver(k, lax.rem(z + d, Z), z).wait_send()

    @pl.when(z == 0)
    def _():
        for c2 in range(1, C):
            pl.when(c < c2)(total_copy(c2, c).wait_send)
        for block in range(1, Z):
            above_copy(block).wait_send()


def per_device(dims, tracers, eastward, northward, surface_height, sea_mask, mixing, sunlight, reaction):
    C, H, Z, levels = dims
    group, rows, cols = eastward.shape
    half = TILE // 2
    first_level = lax.axis_index(("comp", "trc")) * group
    keep = (first_level + jnp.arange(group) < levels - 1).astype(jnp.float32)[:, None, None]
    wet = sea_mask.astype(jnp.float32)
    stacked = jnp.concatenate([eastward, northward, mixing, surface_height[None], wet[None]], 0)
    edges = with_halo(stacked, (("horiz", 1),), half + 2)
    east, north, flux_x, flux_y, kappa = ocean_step(
        edges[:group], edges[group : 2 * group], edges[3 * group], edges[3 * group + 1],
        edges[2 * group : 3 * group, 2:-2], keep,
    )
    coef = jnp.stack([flux_x[:, 1:], flux_y, kappa])
    coef = jnp.concatenate([coef[:, :, half:], coef[:, :, :half]], 2)
    wide, deep, f32 = rows + TILE, group * Z, jnp.float32
    dma = pltpu.SemaphoreType.DMA
    vmem = pl.BlockSpec(memory_space=pltpu.VMEM)
    tracers_out, heating = pl.pallas_call(
        functools.partial(kernel, dims),
        out_shape=(
            jax.ShapeDtypeStruct((C * Z, group, rows, cols), f32),
            jax.ShapeDtypeStruct((group, rows, cols), f32),
        ),
        in_specs=[pl.BlockSpec(memory_space=pl.ANY), vmem, vmem, pl.BlockSpec(memory_space=pltpu.SMEM)],
        out_specs=(vmem, vmem),
        scratch_shapes=[
            pltpu.VMEM((SUBSTEPS + 1, C, deep + 2, wide, cols), f32),
            pltpu.VMEM((2, C, deep + 2, TILE, cols), f32),
            pltpu.VMEM((C * Z, group, rows, cols), f32),
            pltpu.VMEM((3, deep + 1, wide, cols), f32),
            pltpu.VMEM((rows, cols), f32),
            pltpu.VMEM((C, rows, cols), f32),
            pltpu.VMEM((Z, rows, cols), f32),
            pltpu.VMEM((rows, cols), f32),
            dma((C, 3)), dma((1,)), dma((C, 3)),
            dma((2, Z)), dma((Z,)),
            dma((1,)), dma((1,)),
            dma((SUBSTEPS, C, 2)), dma((SUBSTEPS, C, 2)),
            dma((C, Z)), dma((C, Z)),
            dma((C,)), dma((C,)),
            dma((Z,)), dma((1,)),
        ],
        compiler_params=pltpu.CompilerParams(
            collective_id=0, has_side_effects=True, vmem_limit_bytes=48 * 1024 * 1024
        ),
    )(tracers, coef, sunlight, reaction)
    return (east[:, half : half + rows], north[:, half : half + rows], tracers_out, heating)


def solution(mesh):
    C, H, Z = (mesh.shape[a] for a in ("comp", "horiz", "trc"))

    def local(tracers, eastward, *rest):
        dims = (C, H, Z, eastward.shape[0] * C * Z)
        return per_device(dims, tracers, eastward, *rest)

    return jax.shard_map(
        local,
        mesh=mesh,
        in_specs=(
            P(("comp", "trc"), None, "horiz", None),
            P(("comp", "trc"), "horiz", None),
            P(("comp", "trc"), "horiz", None),
            P("horiz", None),
            P("horiz", None),
            P(("comp", "trc"), "horiz", None),
            P("horiz", None),
            P(),
        ),
        out_specs=(
            P(("comp", "trc"), "horiz", None),
            P(("comp", "trc"), "horiz", None),
            P(None, ("comp", "trc"), "horiz", None),
            P(("comp", "trc"), "horiz", None),
        ),
        check_vma=False,
    )
```

time: 253 us -> 144 us (0.57); the launches traced: 248 us -> 142 us
  Pallas kernels: 0 us -> 123 us
  waiting for transfers between devices: 77.6 us -> 4.18 us
  blocking collectives: 68.8 us -> 0 us
  starting transfers between devices: 69.6 us -> 4.41 us
  other arithmetic: 20.3 us -> 1.68 us
  matrix products: 4.72 us -> 0 us
  local copies, waits for them, and re-layouts: 5.49 us -> 8.29 us
    pallas_call x0 -> x1, Pallas kernels: none -> 123 us  [per_device(): pl.pallas_call(functools.partial(kernel, dims), out_shape=(jax.ShapeDtype...]
    all_gather x1 -> x0, blocking collectives: 68.8 us -> none  [entering(): everything = lax.all_gather(shard, axis)]
    ppermute x9 -> x1, starting transfers between devices: 40.3 us -> 1.29 us  [with_halo(): lax.ppermute(lax.slice_in_dim(block, 0, width, axis=dim), axis, backward)]
    all_to_all x1 -> x0, waiting for transfers between devices: 37.3 us -> none  [per_device(): lax.all_to_all(tracers, ('comp', 'trc'), split_axis=1, concat_axis=0, til...]
    ppermute x9 -> x1, waiting for transfers between devices: 23.2 us -> 0.42 us  [with_halo(): lax.ppermute(lax.slice_in_dim(block, block.shape[dim] - width, None, axis...]
    ppermute x9 -> x1, starting transfers between devices: 21.5 us -> 3.12 us  [with_halo(): lax.ppermute(lax.slice_in_dim(block, block.shape[dim] - width, None, axis...]
    ppermute x9 -> x1, waiting for transfers between devices: 17.1 us -> 3.77 us  [with_halo(): lax.ppermute(lax.slice_in_dim(block, 0, width, axis=dim), axis, backward)]
    add x9 -> x0, other arithmetic: 8.2 us -> none  [the longest x4 3.4 us: advance(): jnp.maximum(flux_x, 0.0) * level_mid[..., 0:width + 1, :]]
  transfers between devices with their start and end apart: 20 -> 2, of which waited for: 14 -> 2; matrix products, arithmetic and copies ran while one was open for 2% -> 0% of each run, Pallas kernels for 0% -> 0%
where the time goes in v1:
time: 144 us; the launch traced here: 142 us
  Pallas kernels  123 us (85%)
  local copies, waits for them, and re-layouts  8.29 us (6%)
  starting transfers between devices  4.41 us (3%)
  waiting for transfers between devices  4.18 us (3%)
  other arithmetic  1.68 us (1%)
    pallas_call x1, Pallas kernels, per_device(): pl.pallas_call(functools.partial(kernel, dims), out_shape=(jax.ShapeDtype...  123 us
    unnamed x12, local copies, waits for them, and re-layouts  6.86 us
    ppermute x1, waiting for transfers between devices, with_halo(): lax.ppermute(lax.slice_in_dim(block, 0, width, axis=dim), axis, backward)  3.77 us
    ppermute x1, starting transfers between devices, with_halo(): lax.ppermute(lax.slice_in_dim(block, block.shape[dim] - width, None, axis...  3.12 us
  transfers between devices with their start and end apart: 2, of which 2 were waited for; matrix products, arithmetic and copies ran while one was open for 0% of the time, Pallas kernels for 0%

profile of v1, /device:TPU:29, one launch (start us, length us, event | category | flops | bytes accessed | tf_op | source)
XLA Modules:
  0.0 142.4 jit_solution(13579738818422074978)
XLA Ops:
  0.6 0.9 constant_dynamic-update-slice_fusion.2
  1.5 0.9 constant_dynamic-update-slice_fusion.1
  2.5 0.9 constant_dynamic-update-slice_fusion
  3.4 0.8 bitcast_dynamic-update-slice_fusion.1
  4.2 0.8 bitcast_dynamic-update-slice_fusion
  4.9 3.1 %collective-permute-start = (f32[14,6,256]{2,1,0:T(8,128)S(1)}, f32[14,6,256]{2,1,0:T(8,128)S(1)}, u32[]{:S(2)}, u32[]{:S(2)}) collective-permute-start(f32[14,6,256]{2,1,0:T(8,128)S(1)} %get-tuple-element.18), channel_id=1, source_target_pairs={{0,4},{1,5},{2,6},{3,7},{8,12},{9,13},{10,14},{11,15},{16,20},{17,... | collective-permute-start | bytes 258056 | tf_op jit(solution)/shard_map/ppermute | solution.py:25
  8.1 1.3 collective-permute-start.1
  9.4 0.4 collective-permute-done
  9.8 3.8 %collective-permute-done.1 = f32[14,6,256]{2,1,0:T(8,128)S(1)} collective-permute-done((f32[14,6,256]{2,1,0:T(8,128)S(1)}, f32[14,6,256]{2,1,0:T(8,128)S(1)}, u32[]{:S(2)}, u32[]{:S(2)}) %collective-permute-start.1) | collective-permute-done | bytes 86048 | tf_op jit(solution)/shard_map/ppermute | solution.py:28
  13.6 0.1 pad_maximum_fusion
  13.8 0.3 fusion.8
  14.1 0.7 slice.207
  14.7 0.1 fusion.30
  14.8 0.3 multiply_bitcast_fusion
  15.1 0.7 slice.217
  15.8 0.0 copy-start
  15.8 0.0 copy-start.1
  15.8 0.0 copy-start.2
  15.8 0.1 multiply_bitcast_fusion.1
  16.0 1.4 copy-done
  17.4 0.0 copy-done.1
  17.4 0.0 copy-done.2
  17.4 123.1 %shard_map.111 = (f32[16,4,32,256]{3,2,1,0:T(8,128)S(1)}, f32[4,32,256]{2,1,0:T(8,128)S(1)}) custom-call(f32[1,64,32,256]{3,2,1,0:T(8,128)S(1)} %copy-done, f32[3,4,40,256]{3,2,1,0:T(8,128)S(1)} %fusion.coef, f32[32,256]{1,0:T(8,128)S(1)} %copy-done.1, f32[16,16]{1,0:T(8,128)S(1)} %copy-done.2), custom_call_target="tpu_custom_call" | custom-call | tf_op jit(solution)/shard_map/pallas_call | solution.py:370
  140.4 1.3 copy.18
  141.8 0.7 copy.19
  (11 shorter events, 0.2 us)
Async XLA Ops:
  4.9 4.9 %collective-permute-start = (f32[14,6,256]{2,1,0:T(8,128)S(1)}, f32[14,6,256]{2,1,0:T(8,128)S(1)}, u32[]{:S(2)}, u32[]{:S(2)}) collective-permute-start(f32[14,6,256]{2,1,0:T(8,128)S(1)} %get-tuple-element.18), channel_id=1, source_target_pairs={{0,4},{1,5},{2,6},{3,7},{8,12},{9,13},{10,14},{11,15},{16,20},{17,... | collective-permute-start | bytes 258056 | tf_op jit(solution)/shard_map/ppermute | solution.py:25
  8.1 5.5 %collective-permute-start.1 = (f32[14,6,256]{2,1,0:T(8,128)S(1)}, f32[14,6,256]{2,1,0:T(8,128)S(1)}, u32[]{:S(2)}, u32[]{:S(2)}) collective-permute-start(f32[14,6,256]{2,1,0:T(8,128)S(1)} %get-tuple-element.19), channel_id=1, source_target_pairs={{4,0},{5,1},{6,2},{7,3},{12,8},{13,9},{14,10},{15,11},{20,16},{21,... | collective-permute-start | bytes 258056 | tf_op jit(solution)/shard_map/ppermute | solution.py:28
  15.8 1.6 %copy-start = (f32[1,64,32,256]{3,2,1,0:T(8,128)S(1)}, f32[1,64,32,256]{3,2,1,0:T(8,128)}, u32[]{:S(2)}) copy-start(f32[1,64,32,256]{3,2,1,0:T(8,128)} %tr.1) | copy-start | bytes 6291460
  15.8 1.6 %copy-start.1 = (f32[32,256]{1,0:T(8,128)S(1)}, f32[32,256]{1,0:T(8,128)}, u32[]{:S(2)}) copy-start(f32[32,256]{1,0:T(8,128)} %sun.1) | copy-start | bytes 98308
  15.8 1.6 %copy-start.2 = (f32[16,16]{1,0:T(8,128)S(1)}, f32[16,16]{1,0:T(8,128)}, u32[]{:S(2)}) copy-start(f32[16,16]{1,0:T(8,128)} %react.1) | copy-start | bytes 3076

commit v2 on v1

--- a/solution.py
+++ b/solution.py
@@ -17,75 +17,6 @@
 HALF_LIGHT = 0.3
 
 
-def with_halo(block, sides, width):
-    for axis, dim in sides:
-        count = lax.axis_size(axis)
-        forward = [(i, i + 1) for i in range(count - 1)]
-        backward = [(target, source) for source, target in forward]
-        low = lax.ppermute(
-            lax.slice_in_dim(block, block.shape[dim] - width, None, axis=dim), axis, forward
-        )
-        high = lax.ppermute(lax.slice_in_dim(block, 0, width, axis=dim), axis, backward)
-        block = jnp.concatenate([low, block, high], axis=dim)
-    return block
-
-
-def pad_rows(array):
-    return jnp.pad(array, [(0, 0)] * (array.ndim - 1) + [(1, 1)])
-
-
-def ocean_step(east_ext, north_ext, height_ext, wet_ext, mixing, bottom_keep):
-    width = east_ext.shape[1] - 4
-    rows = east_ext.shape[2]
-    coriolis = 0.5 + 0.5 * jnp.arange(rows, dtype=jnp.float32) / rows
-    east_pad = pad_rows(east_ext)
-    north_pad = pad_rows(north_ext)
-    height_pad = pad_rows(height_ext)
-    wet_pad = pad_rows(wet_ext)
-    east_mid = east_ext[:, 1 : width + 2]
-    east_lap = (
-        east_ext[:, 2 : width + 3]
-        + east_ext[:, 0 : width + 1]
-        + east_pad[:, 1 : width + 2, 2:]
-        + east_pad[:, 1 : width + 2, :-2]
-        - 4.0 * east_mid
-    )
-    north_avg = 0.25 * (
-        north_pad[:, 1 : width + 2, 1:-1]
-        + north_pad[:, 2 : width + 3, 1:-1]
-        + north_pad[:, 1 : width + 2, :-2]
-        + north_pad[:, 2 : width + 3, :-2]
-    )
-    slope_x = height_ext[2 : width + 3] - height_ext[1 : width + 2]
-    open_x = wet_ext[1 : width + 2] * wet_ext[2 : width + 3]
-    east_new = open_x * (
-        east_mid + TIME_STEP * (coriolis * north_avg - GRAVITY * slope_x + VISCOSITY * east_lap)
-    )
-    north_mid = north_ext[:, 2 : width + 2]
-    north_lap = (
-        north_ext[:, 3 : width + 3]
-        + north_ext[:, 1 : width + 1]
-        + north_pad[:, 2 : width + 2, 2:]
-        + north_pad[:, 2 : width + 2, :-2]
-        - 4.0 * north_mid
-    )
-    east_avg = 0.25 * (
-        east_pad[:, 2 : width + 2, 1:-1]
-        + east_pad[:, 1 : width + 1, 1:-1]
-        + east_pad[:, 2 : width + 2, 2:]
-        + east_pad[:, 1 : width + 1, 2:]
-    )
-    slope_y = height_pad[2 : width + 2, 2:] - height_pad[2 : width + 2, 1:-1]
-    open_y = wet_pad[2 : width + 2, 1:-1] * wet_pad[2 : width + 2, 2:]
-    north_new = open_y * (
-        north_mid + TIME_STEP * (-coriolis * east_avg - GRAVITY * slope_y + VISCOSITY * north_lap)
-    )
-    east_out = east_new[:, 1:]
-    speed = jnp.minimum(east_out * east_out + north_new * north_new, 1.0)
-    kappa = wet_ext[2 : width + 2] * mixing * (1.0 + speed) * bottom_keep
-    return (east_out, north_new, COURANT * east_new, COURANT * north_new, kappa)
-
-
 TILE = 8
 MESH = pl.DeviceIdType.MESH
 
@@ -97,17 +28,32 @@
 
 
 def kernel(
-    dims, tr, coef, sun, react, out, heat,
-    T, side, F, CF, tot, totr, pre, abv,
-    ts, tl, trs, cs, cr, ks, kr, hs, hr, zs, zr, us, ur, bs, br,
+    dims, east, north, mix, height, mask, tr, sun, react,
+    east_out, north_out, out, heat,
+    R, T, side, F, CF, W, tot, totr, pre, abv,
+    rs, rr, ts, tl, trs, cs, cr, ks, kr, hs, hr, zs, zr, us, ur, bs, br,
 ):
     C, H, Z, levels = dims
     c, h, z = (lax.axis_index(a) for a in ("comp", "horiz", "trc"))
-    group = coef.shape[1]
+    group = east.shape[0]
     deep = group * Z
     rows, wide = tr.shape[2], T.shape[3]
     cols = tr.shape[3]
     has_left, has_right = h > 0, h < H - 1
+
+    R[pl.ds(0, group), pl.ds(0, rows)] = east[...]
+    R[pl.ds(group, group), pl.ds(0, rows)] = north[...]
+    R[pl.ds(2 * group, group), pl.ds(0, rows)] = mix[...]
+    R[3 * group, pl.ds(0, rows)] = height[...]
+    R[3 * group + 1, pl.ds(0, rows)] = mask[...].astype(jnp.float32)
+
+    @pl.when(h == 0)
+    def _():
+        R[:, pl.ds(rows + TILE, TILE)] = jnp.zeros((R.shape[0], TILE, cols), jnp.float32)
+
+    @pl.when(h == H - 1)
+    def _():
+        R[:, pl.ds(rows, TILE)] = jnp.zeros((R.shape[0], TILE, cols), jnp.float32)
 
     def greet(device):
         pl.semaphore_signal(pltpu.get_barrier_semaphore(), inc=1, device_id=device, device_id_type=MESH)
@@ -127,10 +73,6 @@
         where = pl.ds(1 + block * group, group)
         src = CF.at[:, where]
         return remote(src, CF.at[:, where], cs.at[up, block], cr.at[block], (c, h, z + 1 if up else z - 1))
-
-    CF[:, pl.ds(1 + z * group, group)] = coef[...]
-    pl.when(z < Z - 1)(lambda: coef_copy(1, z).start())
-    pl.when(z > 0)(lambda: coef_copy(0, z).start())
 
     def tracer_copies(target, source, partner):
         low, high = int(target > 0), int(target < C - 1)
@@ -148,12 +90,68 @@
         there = remote(*middle, ts.at[target, 0], trs.at[source, 0], (partner, h, z))
         return here, there, left, right
 
+    to_left = remote(
+        R.at[:, pl.ds(0, TILE)], R.at[:, pl.ds(rows, TILE)], rs.at[0], rr.at[0], (c, h - 1, z))
+    to_right = remote(
+        R.at[:, pl.ds(rows - TILE, TILE)], R.at[:, pl.ds(rows + TILE, TILE)], rs.at[1], rr.at[1], (c, h + 1, z))
+    pl.when(has_left)(to_left.start)
+    pl.when(has_right)(to_right.start)
+
     for c2 in range(C):
         here, there, left, right = tracer_copies(c2, c, c2)
         pl.when(c == c2)(here.start)
         pl.when(c != c2)(there.start)
         pl.when(has_right)(left.start)
         pl.when(has_left)(right.start)
+
+    pl.when(has_right)(to_left.wait_recv)
+    pl.when(has_left)(to_right.wait_recv)
+    ring = rows + 2 * TILE
+    lane = lax.broadcasted_iota(jnp.int32, (ring, cols), 1)
+    coriolis = 0.5 + 0.5 * lane.astype(jnp.float32) / cols
+    sub = lax.broadcasted_iota(jnp.int32, (TILE, cols), 0)
+
+    def next_x(a):
+        return pltpu.roll(a, ring - 1, 0)
+
+    def last_x(a):
+        return pltpu.roll(a, 1, 0)
+
+    def next_y(a):
+        return jnp.where(lane < cols - 1, pltpu.roll(a, cols - 1, 1), 0.0)
+
+    def last_y(a):
+        return jnp.where(lane > 0, pltpu.roll(a, 1, 1), 0.0)
+
+    def pack(which, at, a):
+        CF[which, at, pl.ds(0, rows)] = a[:rows]
+        CF[which, at, pl.ds(rows, TILE)] = jnp.where(
+            sub < TILE // 2, a[rows : rows + TILE], a[rows + TILE :])
+
+    @pl.loop(0, group)
+    def _(l):
+        u, v, eta, wet = R[l], R[group + l], R[3 * group], R[3 * group + 1]
+        u_next, v_last = next_y(u), last_y(v)
+        u_lap = next_x(u) + last_x(u) + u_next + last_y(u) - 4.0 * u
+        v_lap = next_x(v) + last_x(v) + next_y(v) + v_last - 4.0 * v
+        v_pair, u_pair = v + v_last, u + u_next
+        v_avg = 0.25 * (v_pair + next_x(v_pair))
+        u_avg = 0.25 * (u_pair + last_x(u_pair))
+        new_u = wet * next_x(wet) * (
+            u + TIME_STEP * (coriolis * v_avg - GRAVITY * (next_x(eta) - eta) + VISCOSITY * u_lap))
+        new_v = wet * next_y(wet) * (
+            v + TIME_STEP * (-coriolis * u_avg - GRAVITY * (next_y(eta) - eta) + VISCOSITY * v_lap))
+        speed = jnp.minimum(new_u * new_u + new_v * new_v, 1.0)
+        level = z * group + l
+        keep = jnp.where(c * deep + level < levels - 1, 1.0, 0.0)
+        pack(0, 1 + level, COURANT * new_u)
+        pack(1, 1 + level, COURANT * new_v)
+        pack(2, 1 + level, wet * R[2 * group + l] * (1.0 + speed) * keep)
+        east_out[l] = new_u[:rows]
+        north_out[l] = new_v[:rows]
+
+    pl.when(z < Z - 1)(lambda: coef_copy(1, z).start())
+    pl.when(z > 0)(lambda: coef_copy(0, z).start())
 
     @pl.when(h == 0)
     def _():
@@ -182,16 +180,32 @@
             side[0, k, deep + 1] = jnp.zeros((TILE, cols), jnp.float32)
             side[1, k, deep + 1] = jnp.zeros((TILE, cols), jnp.float32)
 
+    def weigh(block):
+        @pl.loop(0, group)
+        def _(i):
+            l = block * group + i
+            fx, fy = CF[0, l + 1], CF[1, l + 1]
+            px, mx = jnp.maximum(fx, 0.0), jnp.minimum(fx, 0.0)
+            py, my = jnp.maximum(fy, 0.0), jnp.minimum(fy, 0.0)
+            W[0, l] = 1.0 + pltpu.roll(mx, 1, 0) - px + pltpu.roll(my, 1, 1) - py
+            W[1, l] = pltpu.roll(px, 1, 0)
+            W[2, l] = -mx
+            W[3, l] = pltpu.roll(py, 1, 1)
+            W[4, l] = -my
+
+    weigh(z)
     for d in range(1, Z):
         @pl.when(z >= d)
         def _():
             coef_copy(1, z - d).wait_recv()
             pl.when(z < Z - 1)(lambda: coef_copy(1, z - d).start())
+            weigh(z - d)
 
         @pl.when(z + d < Z)
         def _():
             coef_copy(0, z + d).wait_recv()
             pl.when(z > 0)(lambda: coef_copy(0, z + d).start())
+            weigh(z + d)
 
     kup = remote(CF.at[2, deep], CF.at[2, 0], ks.at[0], kr.at[0], (c + 1, h, z))
     pl.when(c < C - 1)(kup.start)
@@ -212,8 +226,6 @@
 
     def above_copy(target):
         return remote(pre.at[target], abv, bs.at[target], br.at[0], (c, h, target))
-
-    sub = lax.broadcasted_iota(jnp.int32, (TILE, cols), 0)
 
     def arrive(k):
         for cc in range(C):
@@ -268,16 +280,14 @@
 
         def level(l, carry):
             up, mid, down = T[s, k, l], T[s, k, l + 1], T[s, k, l + 2]
-            fx, fy = CF[0, l + 1], CF[1, l + 1]
-            E = jnp.maximum(fx, 0.0) * mid + jnp.minimum(fx, 0.0) * pltpu.roll(mid, wide - 1, 0)
-            N = jnp.maximum(fy, 0.0) * mid + jnp.minimum(fy, 0.0) * pltpu.roll(mid, cols - 1, 1)
             T[s + 1, k, l + 1] = (
-                mid + (pltpu.roll(E, 1, 0) - E) + (pltpu.roll(N, 1, 1) - N)
-                + CF[2, l + 1] * (down - mid) - CF[2, l] * (mid - up)
+                W[0, l] * mid + W[1, l] * pltpu.roll(mid, 1, 0) + W[2, l] * pltpu.roll(mid, wide - 1, 0)
+                + W[3, l] * pltpu.roll(mid, 1, 1) + W[4, l] * pltpu.roll(mid, cols - 1, 1)
+                + CF[2, l + 1] * (down - mid) + CF[2, l] * (up - mid)
             )
             return carry
 
-        lax.fori_loop(0, deep, level, 0)
+        lax.fori_loop(0, deep, level, 0, unroll=2)
 
         @pl.when(s < SUBSTEPS - 1)
         def _():
@@ -321,6 +331,8 @@
 
     lax.fori_loop(0, group * (rows // TILE), react_tile, 0)
 
+    pl.when(has_left)(to_left.wait_send)
+    pl.when(has_right)(to_right.wait_send)
     pl.when(z < Z - 1)(lambda: coef_copy(1, z).wait_send())
     pl.when(z > 0)(lambda: coef_copy(0, z).wait_send())
     for d in range(1, Z):
@@ -352,38 +364,29 @@
 def per_device(dims, tracers, eastward, northward, surface_height, sea_mask, mixing, sunlight, reaction):
     C, H, Z, levels = dims
     group, rows, cols = eastward.shape
-    half = TILE // 2
-    first_level = lax.axis_index(("comp", "trc")) * group
-    keep = (first_level + jnp.arange(group) < levels - 1).astype(jnp.float32)[:, None, None]
-    wet = sea_mask.astype(jnp.float32)
-    stacked = jnp.concatenate([eastward, northward, mixing, surface_height[None], wet[None]], 0)
-    edges = with_halo(stacked, (("horiz", 1),), half + 2)
-    east, north, flux_x, flux_y, kappa = ocean_step(
-        edges[:group], edges[group : 2 * group], edges[3 * group], edges[3 * group + 1],
-        edges[2 * group : 3 * group, 2:-2], keep,
-    )
-    coef = jnp.stack([flux_x[:, 1:], flux_y, kappa])
-    coef = jnp.concatenate([coef[:, :, half:], coef[:, :, :half]], 2)
     wide, deep, f32 = rows + TILE, group * Z, jnp.float32
     dma = pltpu.SemaphoreType.DMA
     vmem = pl.BlockSpec(memory_space=pltpu.VMEM)
-    tracers_out, heating = pl.pallas_call(
+    plane = jax.ShapeDtypeStruct((group, rows, cols), f32)
+    return pl.pallas_call(
         functools.partial(kernel, dims),
         out_shape=(
-            jax.ShapeDtypeStruct((C * Z, group, rows, cols), f32),
-            jax.ShapeDtypeStruct((group, rows, cols), f32),
+            plane, plane, jax.ShapeDtypeStruct((C * Z, group, rows, cols), f32), plane,
         ),
-        in_specs=[pl.BlockSpec(memory_space=pl.ANY), vmem, vmem, pl.BlockSpec(memory_space=pltpu.SMEM)],
-        out_specs=(vmem, vmem),
+        in_specs=[vmem] * 5 + [pl.BlockSpec(memory_space=pl.ANY), vmem, pl.BlockSpec(memory_space=pltpu.SMEM)],
+        out_specs=(vmem,) * 4,
         scratch_shapes=[
+            pltpu.VMEM((3 * group + 2, rows + 2 * TILE, cols), f32),
             pltpu.VMEM((SUBSTEPS + 1, C, deep + 2, wide, cols), f32),
             pltpu.VMEM((2, C, deep + 2, TILE, cols), f32),
             pltpu.VMEM((C * Z, group, rows, cols), f32),
             pltpu.VMEM((3, deep + 1, wide, cols), f32),
+            pltpu.VMEM((5, deep, wide, cols), f32),
             pltpu.VMEM((rows, cols), f32),
             pltpu.VMEM((C, rows, cols), f32),
             pltpu.VMEM((Z, rows, cols), f32),
             pltpu.VMEM((rows, cols), f32),
+            dma((2,)), dma((2,)),
             dma((C, 3)), dma((1,)), dma((C, 3)),
             dma((2, Z)), dma((Z,)),
             dma((1,)), dma((1,)),
@@ -395,8 +398,7 @@
         compiler_params=pltpu.CompilerParams(
             collective_id=0, has_side_effects=True, vmem_limit_bytes=48 * 1024 * 1024
         ),
-    )(tracers, coef, sunlight, reaction)
-    return (east[:, half : half + rows], north[:, half : half + rows], tracers_out, heating)
+    )(eastward, northward, mixing, surface_height, sea_mask, tracers, sunlight, reaction)
 
 
 def solution(mesh):

time: 144 us -> 113 us (0.78)
  Pallas kernels: 123 us -> 101 us
  starting transfers between devices: 4.41 us -> 0 us
  waiting for transfers between devices: 4.18 us -> 0 us
  local copies, waits for them, and re-layouts: 8.29 us -> 10.5 us
  other arithmetic: 1.68 us -> 0 us
    pallas_call x1, Pallas kernels: 123 us -> 101 us  [per_device(): pl.pallas_call(functools.partial(kernel, dims), out_shape=(plane, plane,...]
    ppermute x2 -> x0, starting transfers between devices: 4.41 us -> none  [the longest x1 3.12 us: with_halo(): lax.ppermute(lax.slice_in_dim(block, block.shape[dim] - width, None, axis...]
    ppermute x2 -> x0, waiting for transfers between devices: 4.18 us -> none  [the longest x1 3.77 us: with_halo(): lax.ppermute(lax.slice_in_dim(block, 0, width, axis=dim), axis, backward)]
    unnamed x12 -> x20, local copies, waits for them, and re-layouts: 6.86 us -> 10.5 us
  transfers between devices with their start and end apart: 2 -> 0, of which waited for: 2 -> 0; matrix products, arithmetic and copies ran while one was open for 0% -> 0% of each run, Pallas kernels for 0% -> 0%
where the time goes in v2:
time: 113 us
  Pallas kernels  101 us (89%)
  local copies, waits for them, and re-layouts  10.5 us (9%)
    pallas_call x1, Pallas kernels, per_device(): pl.pallas_call(functools.partial(kernel, dims), out_shape=(plane, plane,...  101 us
    unnamed x20, local copies, waits for them, and re-layouts  10.5 us

profile of v2, /device:TPU:29, one launch (start us, length us, event | category | flops | bytes accessed | tf_op | source)
XLA Modules:
  0.0 112.5 jit_solution(8783593819289295882)
XLA Ops:
  0.6 0.0 copy-start
  0.6 1.6 %copy-done = f32[1,64,32,256]{3,2,1,0:T(8,128)S(1)} copy-done((f32[1,64,32,256]{3,2,1,0:T(8,128)S(1)}, f32[1,64,32,256]{3,2,1,0:T(8,128)}, u32[]{:S(2)}) %copy-start) | copy-done | bytes 2097176
  2.2 0.0 copy-start.1
  2.2 0.9 copy-done.1
  3.1 0.0 copy-start.2
  3.1 0.9 copy-done.2
  4.0 0.0 copy-start.3
  4.0 0.9 copy-done.3
  4.9 0.0 copy-start.4
  4.9 0.8 copy-done.4
  5.7 0.0 copy-start.5
  5.7 0.8 copy-done.5
  6.5 0.0 copy-start.6
  6.5 0.8 copy-done.6
  7.2 0.0 copy-start.7
  7.2 0.7 copy-done.7
  7.9 101.3 %shard_map.111 = (f32[4,32,256]{2,1,0:T(8,128)S(1)}, f32[4,32,256]{2,1,0:T(8,128)S(1)}, f32[16,4,32,256]{3,2,1,0:T(8,128)S(1)}, f32[4,32,256]{2,1,0:T(8,128)S(1)}) custom-call(f32[4,32,256]{2,1,0:T(8,128)S(1)} %copy-done.1, f32[4,32,256]{2,1,0:T(8,128)S(1)} %copy-done.2, f32[4,32,256]{2,1,0:T(8,128)S(1)} %copy-done.3, f32[32,256]{1,0:T(8,128)S(1)} %copy-done.4, ...), custom_call_target="tpu_custom_call" | custom-call | tf_op jit(solution)/shard_map/pallas_call | solution.py:371
  109.3 0.7 copy.16
  109.9 0.7 copy.17
  110.6 1.3 %copy.18 = f32[16,4,32,256]{3,2,1,0:T(8,128)} copy(f32[16,4,32,256]{3,2,1,0:T(8,128)S(1)} %get-tuple-element.10) | data formatting | bytes 4194304
  111.9 0.7 copy.19
Async XLA Ops:
  0.6 1.6 %copy-start = (f32[1,64,32,256]{3,2,1,0:T(8,128)S(1)}, f32[1,64,32,256]{3,2,1,0:T(8,128)}, u32[]{:S(2)}) copy-start(f32[1,64,32,256]{3,2,1,0:T(8,128)} %tr.1) | copy-start | bytes 6291460
  2.2 0.9 copy-start.1
  3.1 0.9 copy-start.2
  4.0 0.9 copy-start.3
  4.9 0.8 copy-start.4
  5.7 0.8 copy-start.5
  6.5 0.8 copy-start.6
  7.2 0.7 copy-start.7

commit v3 on v2

--- a/solution.py
+++ b/solution.py
@@ -28,10 +28,10 @@
 
 
 def kernel(
-    dims, east, north, mix, height, mask, tr, sun, react,
+    dims, east, north, mix, height, mask, tr, sunlight, react,
     east_out, north_out, out, heat,
-    R, T, side, F, CF, W, tot, totr, pre, abv,
-    rs, rr, ts, tl, trs, cs, cr, ks, kr, hs, hr, zs, zr, us, ur, bs, br,
+    R, sea, sun, T, side, F, CF, W, tot, totr, pre, abv,
+    ls, rs, rr, ts, tl, trs, cs, cr, ks, kr, hs, hr, zs, zr, us, ur, bs, br,
 ):
     C, H, Z, levels = dims
     c, h, z = (lax.axis_index(a) for a in ("comp", "horiz", "trc"))
@@ -41,11 +41,19 @@
     cols = tr.shape[3]
     has_left, has_right = h > 0, h < H - 1
 
-    R[pl.ds(0, group), pl.ds(0, rows)] = east[...]
-    R[pl.ds(group, group), pl.ds(0, rows)] = north[...]
-    R[pl.ds(2 * group, group), pl.ds(0, rows)] = mix[...]
-    R[3 * group, pl.ds(0, rows)] = height[...]
-    R[3 * group + 1, pl.ds(0, rows)] = mask[...].astype(jnp.float32)
+    loads = [
+        pltpu.make_async_copy(src, dst, ls.at[i])
+        for i, (src, dst) in enumerate((
+            (east, R.at[pl.ds(0, group), pl.ds(0, rows)]),
+            (north, R.at[pl.ds(group, group), pl.ds(0, rows)]),
+            (mix, R.at[pl.ds(2 * group, group), pl.ds(0, rows)]),
+            (height, R.at[3 * group, pl.ds(0, rows)]),
+            (mask, sea),
+            (sunlight, sun),
+        ))
+    ]
+    for load in loads:
+        load.start()
 
     @pl.when(h == 0)
     def _():
@@ -89,6 +97,10 @@
         here = pltpu.make_async_copy(*middle, tl.at[0])
         there = remote(*middle, ts.at[target, 0], trs.at[source, 0], (partner, h, z))
         return here, there, left, right
+
+    for load in loads:
+        load.wait()
+    R[3 * group + 1, pl.ds(0, rows)] = sea[...].astype(jnp.float32)
 
     to_left = remote(
         R.at[:, pl.ds(0, TILE)], R.at[:, pl.ds(rows, TILE)], rs.at[0], rr.at[0], (c, h - 1, z))
@@ -199,13 +211,14 @@
         def _():
             coef_copy(1, z - d).wait_recv()
             pl.when(z < Z - 1)(lambda: coef_copy(1, z - d).start())
-            weigh(z - d)
 
         @pl.when(z + d < Z)
         def _():
             coef_copy(0, z + d).wait_recv()
             pl.when(z > 0)(lambda: coef_copy(0, z + d).start())
-            weigh(z + d)
+
+        pl.when(z >= d)(functools.partial(weigh, z - d))
+        pl.when(z + d < Z)(functools.partial(weigh, z + d))
 
     kup = remote(CF.at[2, deep], CF.at[2, 0], ks.at[0], kr.at[0], (c + 1, h, z))
     pl.when(c < C - 1)(kup.start)
@@ -373,10 +386,11 @@
         out_shape=(
             plane, plane, jax.ShapeDtypeStruct((C * Z, group, rows, cols), f32), plane,
         ),
-        in_specs=[vmem] * 5 + [pl.BlockSpec(memory_space=pl.ANY), vmem, pl.BlockSpec(memory_space=pltpu.SMEM)],
+        in_specs=[pl.BlockSpec(memory_space=pltpu.HBM)] * 7 + [pl.BlockSpec(memory_space=pltpu.SMEM)],
         out_specs=(vmem,) * 4,
         scratch_shapes=[
             pltpu.VMEM((3 * group + 2, rows + 2 * TILE, cols), f32),
+            pltpu.VMEM((rows, cols), jnp.int32), pltpu.VMEM((rows, cols), f32),
             pltpu.VMEM((SUBSTEPS + 1, C, deep + 2, wide, cols), f32),
             pltpu.VMEM((2, C, deep + 2, TILE, cols), f32),
             pltpu.VMEM((C * Z, group, rows, cols), f32),
@@ -386,7 +400,7 @@
             pltpu.VMEM((C, rows, cols), f32),
             pltpu.VMEM((Z, rows, cols), f32),
             pltpu.VMEM((rows, cols), f32),
-            dma((2,)), dma((2,)),
+            dma((6,)), dma((2,)), dma((2,)),
             dma((C, 3)), dma((1,)), dma((C, 3)),
             dma((2, Z)), dma((Z,)),
             dma((1,)), dma((1,)),
@@ -396,7 +410,7 @@
             dma((Z,)), dma((1,)),
         ],
         compiler_params=pltpu.CompilerParams(
-            collective_id=0, has_side_effects=True, vmem_limit_bytes=48 * 1024 * 1024
+            collective_id=0, has_side_effects=True, vmem_limit_bytes=63 * 1024 * 1024
         ),
     )(eastward, northward, mixing, surface_height, sea_mask, tracers, sunlight, reaction)
 

time: 113 us -> 112 us (level)
  local copies, waits for them, and re-layouts: 10.5 us -> 6.99 us
  Pallas kernels: 101 us -> 104 us
    unnamed x20 -> x6, local copies, waits for them, and re-layouts: 10.5 us -> 6.99 us
    pallas_call x1, Pallas kernels: 101 us -> 104 us  [per_device(): pl.pallas_call(functools.partial(kernel, dims), out_shape=(plane, plane,...]
where the time goes in v3:
time: 112 us
  Pallas kernels  104 us (93%)
  local copies, waits for them, and re-layouts  6.99 us (6%)
    pallas_call x1, Pallas kernels, per_device(): pl.pallas_call(functools.partial(kernel, dims), out_shape=(plane, plane,...  104 us
    unnamed x6, local copies, waits for them, and re-layouts  6.99 us

profile of v3, /device:TPU:29, one launch (start us, length us, event | category | flops | bytes accessed | tf_op | source)
XLA Modules:
  0.0 111.7 jit_solution(10546715283857008309)
XLA Ops:
  0.6 104.0 %shard_map.111 = (f32[4,32,256]{2,1,0:T(8,128)}, f32[4,32,256]{2,1,0:T(8,128)}, f32[16,4,32,256]{3,2,1,0:T(8,128)}, f32[4,32,256]{2,1,0:T(8,128)}) custom-call(f32[4,32,256]{2,1,0:T(8,128)} %east.1, f32[4,32,256]{2,1,0:T(8,128)} %north.1, f32[4,32,256]{2,1,0:T(8,128)} %mix.1, f32[32,256]{1,0:T(8,128)} %height.1, s32[32,256]{1,0:T(8,128)} %mask.1, ...), custom_call_target="tpu_custom_call" | custom-call | tf_op jit(solution)/shard_map/pallas_call | solution.py:384
  104.7 1.6 %copy.16 = f32[4,32,256]{2,1,0:T(8,128)} copy(f32[4,32,256]{2,1,0:T(8,128)} %get-tuple-element.8) | data formatting | bytes 262144
  106.3 1.6 %copy.17 = f32[4,32,256]{2,1,0:T(8,128)} copy(f32[4,32,256]{2,1,0:T(8,128)} %get-tuple-element.9) | data formatting | bytes 262144
  107.8 0.0 copy-start
  107.8 3.2 %copy.18 = f32[16,4,32,256]{3,2,1,0:T(8,128)} copy(f32[16,4,32,256]{3,2,1,0:T(8,128)} %get-tuple-element.10) | data formatting | bytes 4194304
  111.0 0.0 copy-done
  111.0 0.7 copy.19
Async XLA Ops:
  107.8 3.2 %copy-start = (f32[4,32,256]{2,1,0:T(8,128)S(1)}, f32[4,32,256]{2,1,0:T(8,128)}, u32[]{:S(2)}) copy-start(f32[4,32,256]{2,1,0:T(8,128)} %get-tuple-element.11) | copy-start | bytes 393220

commit v4 on v3

--- a/solution.py
+++ b/solution.py
@@ -109,12 +109,21 @@
     pl.when(has_left)(to_left.start)
     pl.when(has_right)(to_right.start)
 
-    for c2 in range(C):
-        here, there, left, right = tracer_copies(c2, c, c2)
-        pl.when(c == c2)(here.start)
-        pl.when(c != c2)(there.start)
-        pl.when(has_right)(left.start)
-        pl.when(has_left)(right.start)
+    def send_tracer(stage):
+        for cc in range(C):
+            half = max(C // 2, 1)
+            order = sorted(range(C), key=lambda t: (t // half == cc // half, (t - cc) % C))
+            order = [t for t in order if t != cc] + [cc]
+            target = order[stage]
+
+            @pl.when(c == cc)
+            def _():
+                here, there, left, right = tracer_copies(target, cc, target)
+                (here if target == cc else there).start()
+                pl.when(has_right)(left.start)
+                pl.when(has_left)(right.start)
+
+    send_tracer(0)
 
     pl.when(has_right)(to_left.wait_recv)
     pl.when(has_left)(to_right.wait_recv)
@@ -205,6 +214,8 @@
             W[3, l] = pltpu.roll(py, 1, 1)
             W[4, l] = -my
 
+    if C > 1:
+        send_tracer(1)
     weigh(z)
     for d in range(1, Z):
         @pl.when(z >= d)
@@ -217,8 +228,13 @@
             coef_copy(0, z + d).wait_recv()
             pl.when(z > 0)(lambda: coef_copy(0, z + d).start())
 
+        if d + 1 < C:
+            send_tracer(d + 1)
         pl.when(z >= d)(functools.partial(weigh, z - d))
         pl.when(z + d < Z)(functools.partial(weigh, z + d))
+
+    for stage in range(max(Z, 2), C):
+        send_tracer(stage)
 
     kup = remote(CF.at[2, deep], CF.at[2, 0], ks.at[0], kr.at[0], (c + 1, h, z))
     pl.when(c < C - 1)(kup.start)

time: 112 us -> 111 us (level)
  no operation moved by 1% of the time
where the time goes in v4:
time: 111 us
  Pallas kernels  103 us (93%)
  local copies, waits for them, and re-layouts  6.99 us (6%)
    pallas_call x1, Pallas kernels, per_device(): pl.pallas_call(functools.partial(kernel, dims), out_shape=(plane, plane,...  103 us
    unnamed x6, local copies, waits for them, and re-layouts  6.99 us

profile of v4, /device:TPU:29, one launch (start us, length us, event | category | flops | bytes accessed | tf_op | source)
XLA Modules:
  0.0 110.8 jit_solution(2044666800100210891)
XLA Ops:
  0.6 103.1 %shard_map.111 = (f32[4,32,256]{2,1,0:T(8,128)}, f32[4,32,256]{2,1,0:T(8,128)}, f32[16,4,32,256]{3,2,1,0:T(8,128)}, f32[4,32,256]{2,1,0:T(8,128)}) custom-call(f32[4,32,256]{2,1,0:T(8,128)} %east.1, f32[4,32,256]{2,1,0:T(8,128)} %north.1, f32[4,32,256]{2,1,0:T(8,128)} %mix.1, f32[32,256]{1,0:T(8,128)} %height.1, s32[32,256]{1,0:T(8,128)} %mask.1, ...), custom_call_target="tpu_custom_call" | custom-call | tf_op jit(solution)/shard_map/pallas_call | solution.py:400
  103.8 1.6 %copy.16 = f32[4,32,256]{2,1,0:T(8,128)} copy(f32[4,32,256]{2,1,0:T(8,128)} %get-tuple-element.8) | data formatting | bytes 262144
  105.4 1.6 %copy.17 = f32[4,32,256]{2,1,0:T(8,128)} copy(f32[4,32,256]{2,1,0:T(8,128)} %get-tuple-element.9) | data formatting | bytes 262144
  106.9 0.0 copy-start
  106.9 3.2 %copy.18 = f32[16,4,32,256]{3,2,1,0:T(8,128)} copy(f32[16,4,32,256]{3,2,1,0:T(8,128)} %get-tuple-element.10) | data formatting | bytes 4194304
  110.1 0.0 copy-done
  110.1 0.7 copy.19
Async XLA Ops:
  106.9 3.2 %copy-start = (f32[4,32,256]{2,1,0:T(8,128)S(1)}, f32[4,32,256]{2,1,0:T(8,128)}, u32[]{:S(2)}) copy-start(f32[4,32,256]{2,1,0:T(8,128)} %get-tuple-element.11) | copy-start | bytes 393220
